TPU v7x, 256 devices: a whole 4x4x8 slice. The times are simulated.
256 devices in a mesh: blk: 128 (over y, z, x_lo, core), ch: 2 (over x_hi).
Axes of the slice: x: 4 (x_hi: 2, x_lo: 2; x = x_hi * 2 + x_lo), y: 4, z: 8, core: 2. Of those that a mesh axis runs over, the one named last changes fastest.
Arguments:
- record: float32 [4096, 32768], P(('blk', 'ch')), may hold values from -80 to 80, as said below
- templates: bfloat16 [1024, 512, 256], P('blk', 'ch'), may hold values from -0.015625 to 0.015625
- offsets: int32 [1024], P('blk'), may hold values from 0 to 3584
Outputs:
- scores: float32 [1024, 2, 256], P('blk', None, 'ch')
Inputs may be any that keep to these rules, and one draw needn't show every extreme that they name: `record`: finite real samples.
All inputs are finite; a program needn't handle non-finite values.
Results may differ from a plain program's by a relative error of at most 0.0029.
Values may be sent and summed in bfloat16 or wider, within the bound.
A program may use at most 128 MiB of HBM per device.

v0:
```python
import math

import jax
import jax.numpy as jnp
from jax import lax
from jax.sharding import PartitionSpec as P

FRAME = 128
ROT = 2


eps_power = 1e-06
eps_energy = 1e-05
group_width = 8


def shifted(block, axis, distance):
    devices = range(lax.axis_size(axis))
    route = [((i - distance) % len(devices), i) for i in devices]
    return lax.ppermute(block, axis, route)


def dft_tables(frame_len):
    indices = jnp.arange(frame_len, dtype=jnp.int32)
    phases = indices[:, None] * indices[None, :] % frame_len
    angles = phases.astype(jnp.float32) * (2.0 * math.pi / frame_len)
    return (jnp.cos(angles), jnp.sin(angles))


def whiten(chan_block, frame_len):
    chan_count, sample_count = chan_block.shape
    cosine, sine_table = dft_tables(frame_len)
    forward = jnp.concatenate([cosine, -sine_table], axis=1)
    frames = chan_block.reshape(chan_count, sample_count // frame_len, frame_len)
    spectrum = jnp.einsum("cmn,nf->cmf", frames, forward, precision=lax.Precision.HIGHEST)
    real_part = spectrum[:, :, :frame_len]
    imag_part = spectrum[:, :, frame_len:]
    band_power = jnp.mean(real_part * real_part + imag_part * imag_part, axis=1)
    inverse_amp = 1.0 / jnp.sqrt(band_power + eps_power)
    scaled = spectrum * jnp.concatenate([inverse_amp, inverse_amp], axis=1)[:, None, :]
    restored = jnp.einsum("cmf,fn->cmn", scaled, forward.T, precision=lax.Precision.HIGHEST)
    restored = restored / jnp.sqrt(jnp.float32(frame_len))
    return restored.reshape(chan_count, sample_count).astype(jnp.bfloat16)


def diagonal_sums(product, out_len):
    item_count, lag_count, wide_count = product.shape
    flattened = product.reshape(item_count, lag_count * wide_count)
    flattened = jnp.pad(flattened, ((0, 0), (0, lag_count)))
    skewed = flattened.reshape(item_count, lag_count, wide_count + 1)
    return jnp.sum(skewed[:, :, :out_len], axis=1)


def window_energy(power_sum, lag_count, out_len):
    running = jnp.cumsum(power_sum, axis=1)
    running = jnp.pad(running, ((0, 0), (1, 0)))
    return running[:, lag_count : lag_count + out_len] - running[:, :out_len]


def correlate(extended, shapes, starts, out_len):
    shape_count, span_half, lag_count = shapes.shape
    groups = shape_count // group_width
    grouped = shapes.reshape(groups, group_width, span_half, lag_count)
    group_starts = starts.reshape(groups, group_width)

    def one_group(member):
        group_shapes, member_starts = member
        windows = jax.vmap(
            lambda chan_first: lax.dynamic_slice_in_dim(extended, chan_first, span_half, 0)
        )(member_starts)
        product = jnp.einsum(
            "kcs,kcw->ksw", group_shapes, windows, preferred_element_type=jnp.float32
        )
        squares = jnp.square(windows.astype(jnp.float32))
        power_sum = jnp.sum(squares, axis=1)
        return (diagonal_sums(product, out_len), window_energy(power_sum, lag_count, out_len))

    cross_sum, energy = lax.map(one_group, (grouped, group_starts))
    return (cross_sum.reshape(shape_count, out_len), energy.reshape(shape_count, out_len))


def shards(record, templates, offsets):
    whitened = whiten(record, FRAME)
    cycle_size = lax.axis_size("blk")
    my_block = lax.axis_index("blk")
    regrouped = lax.all_to_all(whitened[None], "blk", split_axis=2, concat_axis=0, tiled=True)
    joined = lax.all_gather(regrouped, "ch", axis=1, tiled=True)
    time_slab = joined.reshape(joined.shape[0] * joined.shape[1], joined.shape[2])
    slab_len = time_slab.shape[1]
    span_half = templates.shape[1]
    lag_count = templates.shape[2]
    starts = offsets + lax.axis_index("ch") * span_half
    cross_list = []
    energy_list = []
    held_slab = time_slab
    for visit in range(ROT):
        if visit > 0:
            held_slab = shifted(held_slab, "blk", 1)
        trailing = shifted(held_slab, "blk", -1)
        slab_index = (my_block - visit) % cycle_size
        trailing = jnp.where(slab_index == cycle_size - 1, jnp.zeros_like(trailing), trailing)
        extended = jnp.concatenate([held_slab, trailing], axis=1)
        cross_sum, energy = correlate(extended, templates, starts, slab_len)
        cross_list.append(cross_sum)
        energy_list.append(energy)
    cross_all = jnp.stack(cross_list, axis=1)
    energy_all = jnp.stack(energy_list, axis=1)
    cross_part, energy_part = (
        lax.psum_scatter(cross_all, "ch", scatter_dimension=2, tiled=True),
        lax.psum_scatter(energy_all, "ch", scatter_dimension=2, tiled=True),
    )
    entries = lax.axis_size("ch") * span_half * lag_count
    return cross_part / jnp.sqrt(energy_part / entries + eps_energy)


def solution(mesh):
    return jax.shard_map(
        shards,
        mesh=mesh,
        in_specs=(P(("blk", "ch"), None), P("blk", "ch", None), P("blk")),
        out_specs=P("blk", None, "ch"),
        check_vma=False,
    )
```

profile of v0, /device:TPU:1, one launch (start us, length us, event | category | flops | bytes accessed | tf_op | source)
XLA Modules:
  0.0 586.7 jit_solution(13103600645644479260)
XLA Ops:
  8.9 3.5 convolution_bitcast_fusion.2
  12.7 3.4 multiply_convert_fusion
  17.1 25.0 %copy.35 = bf16[1,16,32768]{1,0,2:T(2,128)(2,1)} copy(bf16[1,16,32768]{2,1,0:T(8,128)(2,1)S(1)} %convert_element_type.36) | data formatting | bytes 2097152 | tf_op jit(solution)/shard_map/convert_element_type | solution.py:43
  42.6 179.1 %reduce.4 = bf16[32768,16]{1,0:T(8,128)(2,1)} reduce(bf16[32768,1,16]{2,1,0:T(2,128)(2,1)} %bitcast.62, bf16[]{:T(256)} %broadcast.95), dimensions={1}, to_apply=%bitcast.46.reduce_sub_computation | reduce | bytes 2097154
  221.8 11.7 %reshape.120 = bf16[128,2,2048]{2,1,0:T(2,128)(2,1)S(1)} reshape(bf16[32768,16]{1,0:T(8,128)(2,1)} %reduce.4) | data formatting | bytes 2097152
  233.4 43.1 %all_to_all.18 = bf16[128,2,2048]{2,1,0:T(2,128)(2,1)S(1)} all-to-all(bf16[128,2,2048]{2,1,0:T(2,128)(2,1)S(1)} %reshape.120), channel_id=1, replica_groups=mesh['blk'=128,'ch'=2] {'blk'}, dimensions={0} | all-to-all | bytes 2097152 | tf_op jit(solution)/shard_map/all_to_all | solution.py:86
  276.5 29.8 %reshape.121 = bf16[32768,1,16]{2,1,0:T(2,128)(2,1)} reshape(bf16[128,2,2048]{2,1,0:T(2,128)(2,1)S(1)} %all_to_all.18) | data formatting | bytes 2097152
  306.3 29.6 %copy.36 = bf16[1,16,32768]{2,1,0:T(8,128)(2,1)S(1)} copy(bf16[1,16,32768]{1,0,2:T(2,128)(2,1)} %bitcast.63) | data formatting | bytes 2097152 | tf_op jit(solution)/shard_map/all_to_all | solution.py:86
  337.4 36.6 %all-gather.3.cloned.1.call-done = bf16[128,1,32,256]{3,0,1,2:T(8,128)(2,1)} async-done(((bf16[128,1,16,256]{3,0,1,2:T(8,128)(2,1)}), bf16[128,1,32,256]{3,0,1,2:T(8,128)(2,1)}) %all-gather.3.cloned.1.call-update) | async-done | bytes 2097168 | tf_op jit(solution)/shard_map/all_gather | solution.py:87
  373.9 2.8 copy.38
  378.5 46.3 %collective-permute-done = bf16[4096,256]{1,0:T(8,128)(2,1)} collective-permute-done((bf16[4096,256]{1,0:T(8,128)(2,1)S(1)}, bf16[4096,256]{1,0:T(8,128)(2,1)}, u32[]{:S(2)}, u32[]{:S(2)}) %collective-permute-start) | collective-permute-done | bytes 2097184 | tf_op jit(solution)/shard_map/ppermute | solution.py:20
  428.8 17.6 %collective-permute-done.1 = bf16[4096,256]{1,0:T(8,128)(2,1)} collective-permute-done((bf16[4096,256]{1,0:T(8,128)(2,1)S(1)}, bf16[4096,256]{1,0:T(8,128)(2,1)}, u32[]{:S(2)}, u32[]{:S(2)}) %collective-permute-start.1) | collective-permute-done | bytes 2097184 | tf_op jit(solution)/shard_map/ppermute | solution.py:20
  446.8 18.1 %while.2 = (s32[]{:T(128)}, bf16[4096,512]{1,0:T(8,128)(2,1)}, s32[8,2]{0,1:T(2,128)S(1)}, bf16[8,256,512]{2,1,0:T(8,128)(2,1)S(1)}, s32[]{:T(128)}) while((s32[]{:T(128)}, bf16[4096,512]{1,0:T(8,128)(2,1)}, s32[8,2]{0,1:T(2,128)S(1)}, bf16[8,256,512]{2,1,0:T(8,128)(2,1)S(1)}, s32[]{:T(128)}) %tuple.35), condition=%wide.while_cond, body=%wide.while_body.sunk | while | flops 2 | bytes 524393 | solution.py:69
  467.7 5.3 copy.40
  473.0 4.6 copy.48
  479.8 9.2 %reshape.70 = f32[8,256,513]{2,1,0:T(8,128)} reshape(f32[8,131328]{1,0:T(8,128)} %pad.19) | data formatting | bytes 8404992 | tf_op jit(solution)/shard_map/while/body/eval_jaxpr/reshape | solution.py:50
  494.4 3.9 pad_maximum_fusion.1
  498.4 18.0 %while.3 = (s32[]{:T(128)}, bf16[4096,512]{1,0:T(8,128)(2,1)}, s32[8,2]{0,1:T(2,128)S(1)}, bf16[8,256,512]{2,1,0:T(8,128)(2,1)S(1)}, s32[]{:T(128)}) while((s32[]{:T(128)}, bf16[4096,512]{1,0:T(8,128)(2,1)}, s32[8,2]{0,1:T(2,128)S(1)}, bf16[8,256,512]{2,1,0:T(8,128)(2,1)S(1)}, s32[]{:T(128)}) %tuple.44), condition=%wide.while_cond.1, body=%wide.while_body.1.sunk | while | flops 2 | bytes 524393 | solution.py:69
  516.5 2.8 convolution_bitcast_fusion
  519.7 5.5 copy.42
  525.2 4.6 copy.49
  532.0 9.2 %reshape.72 = f32[8,256,513]{2,1,0:T(8,128)} reshape(f32[8,131328]{1,0:T(8,128)} %pad.20) | data formatting | bytes 8404992 | tf_op jit(solution)/shard_map/while/body/eval_jaxpr/reshape | solution.py:50
  545.7 14.6 %reduce-scatter.3.cloned.1.call-done = f32[8,2,128]{2,0,1:T(8,128)} async-done(((f32[8,2,256]{2,0,1:T(8,128)}), f32[8,2,128]{2,0,1:T(8,128)}) %reduce-scatter.3.cloned.1.call-update) | async-done | bytes 8208 | tf_op jit(solution)/shard_map/reduce_scatter | solution.py:109
  560.3 18.3 %reduce-scatter.5.cloned.1.call-done = f32[8,2,128]{2,0,1:T(8,128)} async-done(((f32[8,2,256]{2,0,1:T(8,128)}), f32[8,2,128]{2,0,1:T(8,128)}) %reduce-scatter.5.cloned.1.call-update) | async-done | bytes 8208 | tf_op jit(solution)/shard_map/reduce_scatter | solution.py:110
  (101 shorter events, 66.4 us)
Async XLA Ops:
  6.5 458.4 %copy-start = (bf16[8,256,256]{2,1,0:T(8,128)(2,1)S(1)}, bf16[8,256,256]{2,1,0:T(8,128)(2,1)}, u32[]{:S(2)}) copy-start(bf16[8,256,256]{2,1,0:T(8,128)(2,1)} %param.4) | copy-start | bytes 3145732
  6.5 367.4 %all-gather.3.cloned.1.call-start = ((), (), s32[]{:S(2)}) async-start(), calls=%async_computation.5 | async-start | bytes 3145728 | tf_op jit(solution)/shard_map/all_gather | solution.py:87
  337.3 41.2 %copy-start.1 = (s32[8]{0:T(128)S(1)}, s32[8]{0:T(128)}, u32[]{:S(2)}) copy-start(s32[8]{0:T(128)} %param.5) | copy-start | bytes 100
  337.3 223.0 %reduce-scatter.3.cloned.1.call-start = ((), (), s32[]{:S(2)}) async-start(), calls=%async_computation.3 | async-start | bytes 24576 | tf_op jit(solution)/shard_map/reduce_scatter | solution.py:109
  376.7 48.1 %collective-permute-start = (bf16[4096,256]{1,0:T(8,128)(2,1)S(1)}, bf16[4096,256]{1,0:T(8,128)(2,1)}, u32[]{:S(2)}, u32[]{:S(2)}) collective-permute-start(bf16[4096,256]{1,0:T(8,128)(2,1)S(1)} %bitcast.69), channel_id=1, source_target_pairs={{2,0},{4,2},{6,4},{8,6},{10,8},{12,10},{14,12},{16,14},{18,16},{20... | collective-permute-start | bytes 6291464 | tf_op jit(solution)/shard_map/ppermute | solution.py:20
  377.4 69.0 %collective-permute-start.1 = (bf16[4096,256]{1,0:T(8,128)(2,1)S(1)}, bf16[4096,256]{1,0:T(8,128)(2,1)}, u32[]{:S(2)}, u32[]{:S(2)}) collective-permute-start(bf16[4096,256]{1,0:T(8,128)(2,1)S(1)} %bitcast.70), channel_id=1, source_target_pairs={{254,0},{0,2},{2,4},{4,6},{6,8},{8,10},{10,12},{12,14},{14,16},{16... | collective-permute-start | bytes 6291464 | tf_op jit(solution)/shard_map/ppermute | solution.py:20
  446.4 46.2 %collective-permute-start.2 = (bf16[4096,256]{1,0:T(8,128)(2,1)}, bf16[4096,256]{1,0:T(8,128)(2,1)}, u32[]{:S(2)}, u32[]{:S(2)}) collective-permute-start(bf16[4096,256]{1,0:T(8,128)(2,1)} %collective-permute-done.1), channel_id=1, source_target_pairs={{2,0},{4,2},{6,4},{8,6},{10,8},{12,10},{14,12},{16,14},{18,16},{20... | collective-permute-start | bytes 6291464 | tf_op jit(solution)/shard_map/ppermute | solution.py:20
  543.5 35.1 %reduce-scatter.5.cloned.1.call-start = ((), (), s32[]{:S(2)}) async-start(), calls=%async_computation.4 | async-start | bytes 24576 | tf_op jit(solution)/shard_map/reduce_scatter | solution.py:110
Sparse Core Ops, SparseCore 0:
  337.4 36.4 all-gather.2
  543.7 16.6 reduce-scatter.2
  562.8 15.7 reduce-scatter.4
where the time goes:
time: 595 us; the launch traced here: 587 us
  other arithmetic  198 us (33%)
  local copies, waits for them, and re-layouts  184 us (31%)
  waiting for transfers between devices  133 us (22%)
  blocking collectives  43.1 us (7%)
  between operations  13.5 us (2%)
  matrix products  12.5 us (2%)
    unnamed x1, other arithmetic  179 us
    ppermute x3, waiting for transfers between devices, shifted(): return lax.ppermute(block, axis, route)  63.9 us
    unnamed x13, local copies, waits for them, and re-layouts  53.8 us
    all_to_all x1, blocking collectives, shards(): lax.all_to_all(whitened[None], 'blk', split_axis=2, concat_axis=0, tiled=...  43.1 us
    all_gather x1, waiting for transfers between devices, shards(): joined = lax.all_gather(regrouped, 'ch', axis=1, tiled=True)  36.6 us
    gather x48, local copies, waits for them, and re-layouts  35.9 us
    all_to_all x2, local copies, waits for them, and re-layouts, shards(): lax.all_to_all(whitened[None], 'blk', split_axis=2, concat_axis=0, tiled=...  30.7 us
    convert_element_type x2, local copies, waits for them, and re-layouts, whiten(): return restored.reshape(chan_count, sample_count).astype(jnp.bfloat16)  26 us
  transfers between devices with their start and end apart: 6, of which 5 were waited for; matrix products, arithmetic and copies ran while one was open for 9% of the time, Pallas kernels for 0%

commit v1 on v0

v1 whole, which is shorter than its diff:
```python
import functools

import jax
import jax.numpy as jnp
import numpy as np
from jax import lax
from jax.experimental import pallas as pl
from jax.experimental.pallas import tpu as pltpu
from jax.sharding import PartitionSpec as P

MESH = pl.DeviceIdType.MESH
F32 = jnp.float32
BF16 = jnp.bfloat16

FRAME = 128
CHUNK = 16
CSPAN = 512
TLEN = 256
SLAB = 256
TD = 8
GROUP = 4
SUBS = 8
FOLD = 64
EPS_POWER = 1e-6
EPS_ENERGY = 1e-5


def transform_tables():
    n = np.arange(FRAME)
    col = np.arange(FRAME)
    freq = np.where(col <= 64, col, col - 64)
    angle = 2.0 * np.pi * ((n[:, None] * freq[None, :]) % FRAME) / FRAME
    basis = np.where(col <= 64, np.cos(angle), np.sin(angle))
    weight = np.where((col == 0) | (col == 64), 1.0, 2.0) / np.sqrt(FRAME)

    def split(table):
        high = table.astype(jnp.bfloat16)
        low = (table - high.astype(np.float64)).astype(jnp.bfloat16)
        top = np.concatenate([high, low], axis=1)
        bottom = np.concatenate([high, np.zeros_like(high)], axis=1)
        return np.concatenate([top, bottom], axis=0)

    return split(basis), split((basis * weight).T)


def split_rows(value):
    high = value.astype(BF16)
    low = (value - high.astype(F32)).astype(BF16)
    return jnp.concatenate([high, low], axis=1)


def left(value, count):
    return pltpu.roll(value, value.shape[1] - count, 1)


def kernel(
    ng, x_ref, t_ref, off_ref, wf_ref, wi_ref, o_ref,
    ys, ws, wz, wv, tsend, trecv, thalo, lhs, band, offv, offs, cb, qb, hs, hr, rs, rr,
    a_s, a_r, t_s, t_r, f_s, f_r, th_s, th_r, fh_s, fh_r, h_s, h_r, r_s, r_r, loc,
):
    b = lax.axis_index("blk")
    h = lax.axis_index("ch")
    m = lax.div(b, GROUP)
    e = lax.rem(b, GROUP)
    d = 2 * e + h
    up = lax.rem(m + 1, ng)
    down = lax.rem(m + ng - 1, ng)
    rows = CHUNK * ng
    frames = x_ref.shape[1] // FRAME
    wide = GROUP * SLAB

    def peer(sub):
        return {"blk": GROUP * m + lax.div(sub, 2), "ch": lax.rem(sub, 2)}

    def half_block(group):
        return pl.multiple_of(lax.rem(group, 2) * CHUNK, CHUNK)

    def far(group):
        return {"blk": GROUP * group + e}

    bar = pltpu.get_barrier_semaphore()

    def greet_peer(i, carry):
        pl.semaphore_signal(bar, inc=1, device_id=peer(lax.rem(d + i, SUBS)), device_id_type=MESH)
        return carry

    def greet_far(i, carry):
        pl.semaphore_signal(bar, inc=1, device_id=far(lax.rem(m + i, ng)), device_id_type=MESH)
        return carry

    lax.fori_loop(1, SUBS, greet_peer, 0)
    lax.fori_loop(1, ng, greet_far, 0)

    r_id = lax.broadcasted_iota(jnp.int32, (256, 256), 0)
    c_id = lax.broadcasted_iota(jnp.int32, (256, 256), 1)
    slot = 128 * ((r_id >> 4) & 1) + 16 * (r_id >> 5) + (r_id & 15)
    for k in range(TD):
        perm = jnp.where(((slot - c_id - off_ref[k]) & 255) == 0, 1.0, 0.0).astype(BF16)
        placed = jnp.dot(perm, t_ref[k], preferred_element_type=F32).astype(BF16)
        for s in range(SUBS):
            tsend[s, k] = placed[32 * s : 32 * s + 32]

    row8 = lax.broadcasted_iota(jnp.int32, (TD, 128), 0)
    own_off = jnp.zeros((TD, 128), jnp.int32)
    for k in range(TD):
        own_off = jnp.where(row8 == k, off_ref[k], own_off)
    offv[1 + e] = own_off

    pl.semaphore_wait(bar, SUBS - 1 + ng - 1)

    def template_copy(i):
        sub = lax.rem(d + i, SUBS)
        return pltpu.make_async_remote_copy(
            src_ref=tsend.at[sub], dst_ref=trecv.at[d], send_sem=t_s.at[sub], recv_sem=t_r.at[d],
            device_id=peer(sub), device_id_type=MESH,
        )

    def template_arrival(i):
        sub = lax.rem(d + i, SUBS)
        return pltpu.make_async_remote_copy(
            src_ref=tsend.at[sub], dst_ref=trecv.at[sub], send_sem=t_s.at[sub], recv_sem=t_r.at[sub],
            device_id=peer(sub), device_id_type=MESH,
        )

    def offset_copy(i):
        other = lax.rem(e + i, GROUP)
        return pltpu.make_async_remote_copy(
            src_ref=offv.at[1 + e], dst_ref=offv.at[1 + e], send_sem=f_s.at[other], recv_sem=f_r.at[e],
            device_id={"blk": GROUP * m + other}, device_id_type=MESH,
        )

    def offset_arrival(i):
        other = lax.rem(e + i, GROUP)
        return pltpu.make_async_remote_copy(
            src_ref=offv.at[1 + e], dst_ref=offv.at[1 + other], send_sem=f_s.at[other], recv_sem=f_r.at[other],
            device_id={"blk": GROUP * m + other}, device_id_type=MESH,
        )

    for i in range(1, GROUP):
        offset_copy(i).start()

    def start_template(i, carry):
        template_copy(i).start()
        return carry

    lax.fori_loop(1, SUBS, start_template, 0)

    step = 16
    wf = wf_ref[...]

    def forward(i, total):
        part = x_ref[:, pl.ds(pl.multiple_of(i * (step * FRAME), FRAME), step * FRAME)]
        stacked = jnp.concatenate([part[:, f * FRAME : (f + 1) * FRAME] for f in range(step)], axis=0)
        both = jnp.dot(split_rows(stacked), wf, preferred_element_type=F32)
        spec = both[:, :FRAME] + both[:, FRAME:]
        ys[pl.ds(pl.multiple_of(i * (step * CHUNK), 8), step * CHUNK), :] = spec
        return total + jnp.sum((spec * spec).reshape(step, CHUNK, FRAME), axis=0)

    total = lax.fori_loop(0, frames // step, forward, jnp.zeros((CHUNK, FRAME), F32))
    mean = total * (1.0 / frames)
    lane = lax.broadcasted_iota(jnp.int32, (CHUNK, FRAME), 1)
    power = jnp.where((lane & 63) == 0, mean, mean + pltpu.roll(mean, 64, 1))
    amp = 1.0 / jnp.sqrt(power + EPS_POWER)
    wi = wi_ref[...]

    def sample_copy(t):
        return pltpu.make_async_remote_copy(
            src_ref=ws.at[:, pl.ds(pl.multiple_of(t * wide, FRAME), wide)],
            dst_ref=wz.at[lax.div(m, 2), pl.ds(half_block(m), CHUNK), pl.ds(SLAB, wide)],
            send_sem=a_s.at[t], recv_sem=a_r.at[m], device_id=far(t), device_id_type=MESH,
        )

    def sample_arrival(t):
        return pltpu.make_async_remote_copy(
            src_ref=ws.at[:, pl.ds(pl.multiple_of(t * wide, FRAME), wide)],
            dst_ref=wz.at[lax.div(t, 2), pl.ds(half_block(t), CHUNK), pl.ds(SLAB, wide)],
            send_sem=a_s.at[t], recv_sem=a_r.at[t], device_id=far(t), device_id_type=MESH,
        )

    def back(i, carry):
        pair = lax.rem(lax.div(m, 2) + i, ng // 2)
        spec = ys[pl.ds(pl.multiple_of(pair * (step * CHUNK), 8), step * CHUNK), :]
        scaled = (spec.reshape(step, CHUNK, FRAME) * amp[None]).reshape(step * CHUNK, FRAME)
        both = jnp.dot(split_rows(scaled), wi, preferred_element_type=F32)
        white = (both[:, :FRAME] + both[:, FRAME:]).astype(BF16)
        for f in range(step):
            at = pl.multiple_of((pair * step + f) * FRAME, FRAME)
            ws[:, pl.ds(at, FRAME)] = white[f * CHUNK : (f + 1) * CHUNK]
        for q in range(2):
            t = 2 * pair + q

            @pl.when(t != m)
            def _():
                sample_copy(t).start()

        return carry

    lax.fori_loop(0, ng // 2, back, 0)

    wz[:, :, 0:SLAB] = jnp.zeros((rows // 32, 32, SLAB), BF16)
    wz[:, :, SLAB + wide : 2 * SLAB + wide] = jnp.zeros((rows // 32, 32, SLAB), BF16)
    wz[lax.div(m, 2), pl.ds(half_block(m), CHUNK), pl.ds(SLAB, wide)] = ws[
        :, pl.ds(pl.multiple_of(m * wide, FRAME), wide)
    ]
    trecv[d] = tsend[d]

    for i in range(1, GROUP):
        offset_arrival(i).wait()

    def end_template(i, carry):
        template_arrival(i).wait()
        return carry

    lax.fori_loop(1, SUBS, end_template, 0)

    def halo(side, kind):
        group = up if side == 0 else down
        first = SUBS - 2 if side == 0 else 0
        shard = GROUP if side == 0 else 1
        if kind == "t":
            src, dst, sems = trecv.at[pl.ds(first, 2)], thalo.at[side], (th_s, th_r)
        elif kind == "f":
            src, dst, sems = offv.at[shard], offv.at[(GROUP + 1) * side], (fh_s, fh_r)
        else:
            src, dst, sems = hs.at[side], hr.at[side], (h_s, h_r)
            group = down if side == 0 else up
        return pltpu.make_async_remote_copy(
            src_ref=src, dst_ref=dst, send_sem=sems[0].at[side], recv_sem=sems[1].at[side],
            device_id=far(group), device_id_type=MESH,
        )

    for side in range(2):
        halo(side, "f").start()
        halo(side, "t").start()

    w_id = lax.broadcasted_iota(jnp.int32, band.shape, 0)
    l_id = lax.broadcasted_iota(jnp.int32, band.shape, 1)
    gap = w_id - l_id
    band[...] = jnp.where((gap >= 0) & (gap < TLEN), 1.0, 0.0).astype(BF16)

    r_id = lax.broadcasted_iota(jnp.int32, (FOLD, TLEN), 0)
    s_id = lax.broadcasted_iota(jnp.int32, (FOLD, TLEN), 1)
    pick = jnp.where((s_id & (FOLD - 1)) == ((r_id & ~7) + 7 - (r_id & 7)), 1.0, 0.0).astype(BF16)
    part = lax.broadcasted_iota(jnp.int32, (2 * FOLD * 2, TLEN), 1) >> 6
    which = lax.broadcasted_iota(jnp.int32, (2 * FOLD * 2, TLEN), 0) >> 6
    keep = jnp.where(part == which, 1.0, 0.0).astype(BF16)

    def left_operand(first, second):
        both = jnp.concatenate([first, second], axis=0)
        spread = jnp.concatenate([both] * 4, axis=0) * keep
        turned = lax.dot_general(pick, spread, (((1,), (1,)), ((), ())), preferred_element_type=F32)
        return turned.astype(BF16)

    def prepare(q, carry):
        shard = lax.div(q, TD)
        k = lax.rem(q, TD)
        lhs[TD + q] = left_operand(trecv[2 * shard, k], trecv[2 * shard + 1, k])
        return carry

    lax.fori_loop(0, GROUP * TD, prepare, 0)

    for side in range(2):
        halo(side, "f").wait()
        halo(side, "t").wait()

    def prepare_halo(q, carry):
        side = lax.div(q, TD)
        k = lax.rem(q, TD)
        lhs[side * (GROUP + 1) * TD + k] = left_operand(thalo[side, 0, k], thalo[side, 1, k])
        return carry

    lax.fori_loop(0, 2 * TD, prepare_halo, 0)
    to_scalar = pltpu.make_async_copy(offv, offs, loc.at[0])
    to_scalar.start()
    to_scalar.wait()

    def shift_rows(t):
        at = pl.ds(half_block(t), CHUNK)
        block = wz[lax.div(t, 2), at, :]
        wv[lax.div(t, 2), at, :] = jnp.concatenate([block[:, FOLD:], block[:, :FOLD]], axis=1)

    shift_rows(m)

    def arrive(i, carry):
        t = lax.rem(m + i, ng)
        sample_arrival(t).wait()
        shift_rows(t)
        return carry

    lax.fori_loop(1, ng, arrive, 0)

    def correlate(shard, k, c0, width):
        off = offs[shard, k, 0]
        start = 16 * (off >> 7) + jnp.clip((off & 127) - 16 * d, 0, 16)
        r0 = start >> 5
        r1 = r0 + 1
        r2 = jnp.minimum(r0 + 2, rows // 32 - 1)
        late = lax.broadcasted_iota(jnp.int32, (32, width), 0) < (start & 31)
        cols = pl.ds(c0, width)

        def window(ref):
            b0, b1, b2 = ref[r0, :, cols], ref[r1, :, cols], ref[r2, :, cols]
            return jnp.concatenate([jnp.where(late, b1, b0), jnp.where(late, b2, b1)], axis=0)

        w = window(wz)
        v = window(wv)
        n = width - 128
        right = jnp.concatenate([w[:, :n], v[:, :n], w[:, 128:], v[:, 128:]], axis=0)
        prod = jnp.dot(lhs[shard * TD + k], right, preferred_element_type=F32)
        prod = prod[:32] + left(prod[32:], 32)
        prod = prod[:16] + left(prod[16:], 16)
        prod = prod[:8] + left(prod[8:], 8)
        prod = pltpu.roll(prod, n - 7, 1, stride=1, stride_axis=0)
        wide_w = w.astype(F32)
        return prod[:, : n - 128], jnp.sum((wide_w * wide_w).reshape(8, 8, width), axis=0)

    def window_energy(squares, width):
        high = squares.astype(BF16)
        rest = squares - high.astype(F32)
        mid = rest.astype(BF16)
        low = (rest - mid.astype(F32)).astype(BF16)
        sums = jnp.dot(
            jnp.concatenate([high, mid, low], axis=0), band[:width, : width - SLAB], preferred_element_type=F32
        )
        return sums[:TD] + sums[TD : 2 * TD] + sums[2 * TD :]

    for side in range(2):
        shard = (GROUP + 1) * side

        def edge(k, carry):
            cross, squares = correlate(shard, k, side * wide, 2 * SLAB)
            cb[shard, k, :, :SLAB] = cross
            qb[shard, k, :, : 2 * SLAB] = squares
            return carry

        lax.fori_loop(0, TD, edge, 0)
        cross = jnp.sum(cb[shard, :, :, :SLAB], axis=1)
        energy = window_energy(jnp.sum(qb[shard, :, :, : 2 * SLAB], axis=1), 2 * SLAB)
        if side == 0:
            cross = jnp.where(m == 0, 0.0, cross)
            energy = jnp.where(m == 0, 0.0, energy)
        for half in range(2):
            hs[side, 0, half] = cross[:, half * 128 : (half + 1) * 128]
            hs[side, 1, half] = energy[:, half * 128 : (half + 1) * 128]
        halo(side, "r").start()

    def inner(q, carry):
        shard = 1 + lax.div(q, TD)
        k = lax.rem(q, TD)
        cross, squares = correlate(shard, k, pl.multiple_of((shard - 1) * SLAB, SLAB), 3 * SLAB)
        cb[shard, k] = cross
        qb[shard, k] = squares
        return carry

    lax.fori_loop(0, GROUP * TD, inner, 0)

    def result_copy(sub):
        return pltpu.make_async_remote_copy(
            src_ref=rs.at[sub], dst_ref=rr.at[d], send_sem=r_s.at[sub], recv_sem=r_r.at[d],
            device_id=peer(sub), device_id_type=MESH,
        )

    def result_arrival(sub):
        return pltpu.make_async_remote_copy(
            src_ref=rs.at[sub], dst_ref=rr.at[sub], send_sem=r_s.at[sub], recv_sem=r_r.at[sub],
            device_id=peer(sub), device_id_type=MESH,
        )

    for side in range(2):
        halo(side, "r").wait()

    for own in range(GROUP):
        cross = jnp.sum(cb[1 + own], axis=1)
        energy = window_energy(jnp.sum(qb[1 + own], axis=1), 3 * SLAB)
        for tile in range(4):
            visit, half = 1 - tile // 2, tile % 2
            values = [v[:, tile * 128 : (tile + 1) * 128] for v in (cross, energy)]
            for kind in range(2):
                value = values[kind]
                if own == 0 and visit == 1:
                    value = jnp.where(m == 0, 0.0, value) + hr[1, kind, half]
                if own == GROUP - 1 and visit == 0:
                    value = value + hr[0, kind, half]
                rs[2 * own + half, kind, visit] = value

    def start_result(i, carry):
        result_copy(lax.rem(d + i, SUBS)).start()
        return carry

    def end_result(i, carry):
        result_arrival(lax.rem(d + i, SUBS)).wait()
        return carry

    lax.fori_loop(1, SUBS, start_result, 0)
    rr[d] = rs[d]
    lax.fori_loop(1, SUBS, end_result, 0)
    summed = rr[0]
    for sub in range(1, SUBS):
        summed = summed + rr[sub]
    score = summed[0] / jnp.sqrt(summed[1] / (CSPAN * TLEN) + EPS_ENERGY)
    for visit in range(2):
        o_ref[:, visit, :] = score[visit]


def shards(record, templates, offsets):
    ng = lax.axis_size("blk") // GROUP
    samples = record.shape[1]
    rows = CHUNK * ng
    buffer = (GROUP + 2) * SLAB
    wf, wi = transform_tables()
    vmem = pl.BlockSpec(memory_space=pltpu.VMEM)
    dma = pltpu.SemaphoreType.DMA
    return pl.pallas_call(
        functools.partial(kernel, ng),
        out_shape=jax.ShapeDtypeStruct((TD, 2, SLAB // 2), F32),
        in_specs=[vmem, vmem, pl.BlockSpec(memory_space=pltpu.SMEM), vmem, vmem],
        out_specs=vmem,
        scratch_shapes=[
            pltpu.VMEM((samples // FRAME * CHUNK, FRAME), F32),
            pltpu.VMEM((CHUNK, samples), BF16),
            pltpu.VMEM((rows // 32, 32, buffer), BF16),
            pltpu.VMEM((rows // 32, 32, buffer), BF16),
            pltpu.VMEM((SUBS, TD, 32, TLEN), BF16),
            pltpu.VMEM((SUBS, TD, 32, TLEN), BF16),
            pltpu.VMEM((2, 2, TD, 32, TLEN), BF16),
            pltpu.VMEM(((GROUP + 2) * TD, FOLD, 256), BF16),
            pltpu.VMEM((3 * SLAB, 2 * SLAB), BF16),
            pltpu.VMEM((GROUP + 2, TD, 128), jnp.int32),
            pltpu.SMEM((GROUP + 2, TD, 128), jnp.int32),
            pltpu.VMEM((GROUP + 2, TD, 8, 2 * SLAB), F32),
            pltpu.VMEM((GROUP + 2, TD, 8, 3 * SLAB), F32),
            pltpu.VMEM((2, 2, 2, TD, 128), F32),
            pltpu.VMEM((2, 2, 2, TD, 128), F32),
            pltpu.VMEM((SUBS, 2, 2, TD, 128), F32),
            pltpu.VMEM((SUBS, 2, 2, TD, 128), F32),
            dma((ng,)), dma((ng,)), dma((SUBS,)), dma((SUBS,)), dma((GROUP,)), dma((GROUP,)),
            dma((2,)), dma((2,)), dma((2,)), dma((2,)), dma((2,)), dma((2,)), dma((SUBS,)), dma((SUBS,)),
            dma((1,)),
        ],
        compiler_params=pltpu.CompilerParams(
            collective_id=0, has_side_effects=True, vmem_limit_bytes=48 * 2**20
        ),
    )(record, templates, offsets, jnp.asarray(wf), jnp.asarray(wi))


def solution(mesh):
    return jax.shard_map(
        shards,
        mesh=mesh,
        in_specs=(P(("blk", "ch"), None), P("blk", "ch", None), P("blk")),
        out_specs=P("blk", None, "ch"),
        check_vma=False,
    )
```

time: 595 us -> 87.2 us (0.15); the launches traced: 587 us -> 87.1 us
  other arithmetic: 198 us -> 0 us
  local copies, waits for them, and re-layouts: 184 us -> 5.88 us
  waiting for transfers between devices: 133 us -> 0 us
  Pallas kernels: 0 us -> 81.2 us
  blocking collectives: 43.1 us -> 0 us
  between operations: 13.5 us -> 0.01 us
  matrix products: 12.5 us -> 0 us
    unnamed x1 -> x0, other arithmetic: 179 us -> none
    pallas_call x0 -> x1, Pallas kernels: none -> 81.2 us  [shards(): pl.pallas_call(functools.partial(kernel, ng), out_shape=jax.ShapeDtypeStr...]
    ppermute x3 -> x0, waiting for transfers between devices: 63.9 us -> none  [shifted(): return lax.ppermute(block, axis, route)]
    unnamed x13 -> x11, local copies, waits for them, and re-layouts: 53.8 us -> 5.88 us
    all_to_all x1 -> x0, blocking collectives: 43.1 us -> none  [shards(): lax.all_to_all(whitened[None], 'blk', split_axis=2, concat_axis=0, tiled=...]
    all_gather x1 -> x0, waiting for transfers between devices: 36.6 us -> none  [shards(): joined = lax.all_gather(regrouped, 'ch', axis=1, tiled=True)]
    gather x48 -> x0, local copies, waits for them, and re-layouts: 35.9 us -> none
    reduce_scatter x2 -> x0, waiting for transfers between devices: 32.9 us -> none  [the longest x1 18.3 us: shards(): lax.psum_scatter(energy_all, 'ch', scatter_dimension=2, tiled=True)]
  transfers between devices with their start and end apart: 6 -> 0, of which waited for: 5 -> 0; matrix products, arithmetic and copies ran while one was open for 9% -> 0% of each run, Pallas kernels for 0% -> 0%
where the time goes in v1:
time: 87.2 us; the launch traced here: 87.1 us
  Pallas kernels  81.2 us (93%)
  local copies, waits for them, and re-layouts  5.88 us (7%)
    pallas_call x1, Pallas kernels, shards(): pl.pallas_call(functools.partial(kernel, ng), out_shape=jax.ShapeDtypeStr...  81.2 us
    unnamed x11, local copies, waits for them, and re-layouts  5.88 us

profile of v1, /device:TPU:1, one launch (start us, length us, event | category | flops | bytes accessed | tf_op | source)
XLA Modules:
  0.0 87.1 jit_solution(3100088140580481757)
XLA Ops:
  0.0 0.0 copy-start
  0.0 1.6 %copy-done = f32[16,32768]{1,0:T(8,128)S(1)} copy-done((f32[16,32768]{1,0:T(8,128)S(1)}, f32[16,32768]{1,0:T(8,128)}, u32[]{:S(2)}) %copy-start) | copy-done | bytes 2097176
  1.6 0.0 copy-start.1
  1.6 1.2 %copy-done.1 = bf16[8,256,256]{2,1,0:T(8,128)(2,1)S(1)} copy-done((bf16[8,256,256]{2,1,0:T(8,128)(2,1)S(1)}, bf16[8,256,256]{2,1,0:T(8,128)(2,1)}, u32[]{:S(2)}) %copy-start.1) | copy-done | bytes 1048600
  2.8 0.0 copy-start.2
  2.8 0.9 %copy-done.2 = bf16[256,256]{1,0:T(8,128)(2,1)S(1)} copy-done((bf16[256,256]{1,0:T(8,128)(2,1)S(1)}, bf16[256,256]{1,0:T(8,128)(2,1)}, u32[]{:S(2)}) %copy-start.2) | copy-done | bytes 131096
  3.7 0.0 copy-start.3
  3.7 0.9 %copy-done.3 = bf16[256,256]{1,0:T(8,128)(2,1)S(1)} copy-done((bf16[256,256]{1,0:T(8,128)(2,1)S(1)}, bf16[256,256]{1,0:T(8,128)(2,1)}, u32[]{:S(2)}) %copy-start.3) | copy-done | bytes 131096
  4.6 0.0 copy-start.4
  4.6 0.7 copy-done.4
  5.3 81.2 %shard_map.55 = f32[8,2,128]{2,1,0:T(2,128)S(1)} custom-call(f32[16,32768]{1,0:T(8,128)S(1)} %copy-done, bf16[8,256,256]{2,1,0:T(8,128)(2,1)S(1)} %copy-done.1, s32[8]{0:T(128)S(1)} %copy-done.4, bf16[256,256]{1,0:T(8,128)(2,1)S(1)} %copy-done.3, bf16[256,256]{1,0:T(8,128)(2,1)S(1)} %copy-done.2), custom_call_target="tpu_custom_call" | custom-call | tf_op jit(solution)/shard_map/pallas_call | solution.py:413
  86.5 0.6 copy.7
Async XLA Ops:
  0.0 1.6 %copy-start = (f32[16,32768]{1,0:T(8,128)S(1)}, f32[16,32768]{1,0:T(8,128)}, u32[]{:S(2)}) copy-start(f32[16,32768]{1,0:T(8,128)} %x_ref.1) | copy-start | bytes 6291460
  1.6 1.2 %copy-start.1 = (bf16[8,256,256]{2,1,0:T(8,128)(2,1)S(1)}, bf16[8,256,256]{2,1,0:T(8,128)(2,1)}, u32[]{:S(2)}) copy-start(bf16[8,256,256]{2,1,0:T(8,128)(2,1)} %t_ref.1) | copy-start | bytes 3145732
  2.8 0.9 %copy-start.2 = (bf16[256,256]{1,0:T(8,128)(2,1)S(1)}, bf16[256,256]{1,0:T(8,128)(2,1)}, u32[]{:S(2)}) copy-start(bf16[256,256]{1,0:T(8,128)(2,1)} %constant.5.clone.wi_ref) | copy-start | bytes 393220
  3.7 0.9 %copy-start.3 = (bf16[256,256]{1,0:T(8,128)(2,1)S(1)}, bf16[256,256]{1,0:T(8,128)(2,1)}, u32[]{:S(2)}) copy-start(bf16[256,256]{1,0:T(8,128)(2,1)} %constant.4.clone.wf_ref) | copy-start | bytes 393220
  4.6 0.7 copy-start.4

commit v2 on v1

--- a/solution.py
+++ b/solution.py
@@ -156,7 +156,7 @@
         ys[pl.ds(pl.multiple_of(i * (step * CHUNK), 8), step * CHUNK), :] = spec
         return total + jnp.sum((spec * spec).reshape(step, CHUNK, FRAME), axis=0)
 
-    total = lax.fori_loop(0, frames // step, forward, jnp.zeros((CHUNK, FRAME), F32))
+    total = lax.fori_loop(0, frames // step, forward, jnp.zeros((CHUNK, FRAME), F32), unroll=8)
     mean = total * (1.0 / frames)
     lane = lax.broadcasted_iota(jnp.int32, (CHUNK, FRAME), 1)
     power = jnp.where((lane & 63) == 0, mean, mean + pltpu.roll(mean, 64, 1))
@@ -195,7 +195,7 @@
 
         return carry
 
-    lax.fori_loop(0, ng // 2, back, 0)
+    lax.fori_loop(0, ng // 2, back, 0, unroll=8)
 
     wz[:, :, 0:SLAB] = jnp.zeros((rows // 32, 32, SLAB), BF16)
     wz[:, :, SLAB + wide : 2 * SLAB + wide] = jnp.zeros((rows // 32, 32, SLAB), BF16)
@@ -257,7 +257,7 @@
         lhs[TD + q] = left_operand(trecv[2 * shard, k], trecv[2 * shard + 1, k])
         return carry
 
-    lax.fori_loop(0, GROUP * TD, prepare, 0)
+    lax.fori_loop(0, GROUP * TD, prepare, 0, unroll=8)
 
     for side in range(2):
         halo(side, "f").wait()
@@ -269,7 +269,7 @@
         lhs[side * (GROUP + 1) * TD + k] = left_operand(thalo[side, 0, k], thalo[side, 1, k])
         return carry
 
-    lax.fori_loop(0, 2 * TD, prepare_halo, 0)
+    lax.fori_loop(0, 2 * TD, prepare_halo, 0, unroll=8)
     to_scalar = pltpu.make_async_copy(offv, offs, loc.at[0])
     to_scalar.start()
     to_scalar.wait()
@@ -333,7 +333,7 @@
             qb[shard, k, :, : 2 * SLAB] = squares
             return carry
 
-        lax.fori_loop(0, TD, edge, 0)
+        lax.fori_loop(0, TD, edge, 0, unroll=8)
         cross = jnp.sum(cb[shard, :, :, :SLAB], axis=1)
         energy = window_energy(jnp.sum(qb[shard, :, :, : 2 * SLAB], axis=1), 2 * SLAB)
         if side == 0:
@@ -352,7 +352,7 @@
         qb[shard, k] = squares
         return carry
 
-    lax.fori_loop(0, GROUP * TD, inner, 0)
+    lax.fori_loop(0, GROUP * TD, inner, 0, unroll=8)
 
     def result_copy(sub):
         return pltpu.make_async_remote_copy(

time: 87.2 us -> 67.1 us (0.77)
  Pallas kernels: 81.2 us -> 61.1 us
    pallas_call x1, Pallas kernels: 81.2 us -> 61.1 us  [shards(): pl.pallas_call(functools.partial(kernel, ng), out_shape=jax.ShapeDtypeStr...]
where the time goes in v2:
time: 67.1 us; the launch traced here: 67 us
  Pallas kernels  61.1 us (91%)
  local copies, waits for them, and re-layouts  5.88 us (9%)
    pallas_call x1, Pallas kernels, shards(): pl.pallas_call(functools.partial(kernel, ng), out_shape=jax.ShapeDtypeStr...  61.1 us
    unnamed x11, local copies, waits for them, and re-layouts  5.88 us

profile of v2, /device:TPU:1, one launch (start us, length us, event | category | flops | bytes accessed | tf_op | source)
XLA Modules:
  0.0 67.0 jit_solution(16664162475015422271)
XLA Ops:
  0.0 0.0 copy-start
  0.0 1.6 %copy-done = f32[16,32768]{1,0:T(8,128)S(1)} copy-done((f32[16,32768]{1,0:T(8,128)S(1)}, f32[16,32768]{1,0:T(8,128)}, u32[]{:S(2)}) %copy-start) | copy-done | bytes 2097176
  1.6 0.0 copy-start.1
  1.6 1.2 %copy-done.1 = bf16[8,256,256]{2,1,0:T(8,128)(2,1)S(1)} copy-done((bf16[8,256,256]{2,1,0:T(8,128)(2,1)S(1)}, bf16[8,256,256]{2,1,0:T(8,128)(2,1)}, u32[]{:S(2)}) %copy-start.1) | copy-done | bytes 1048600
  2.8 0.0 copy-start.2
  2.8 0.9 %copy-done.2 = bf16[256,256]{1,0:T(8,128)(2,1)S(1)} copy-done((bf16[256,256]{1,0:T(8,128)(2,1)S(1)}, bf16[256,256]{1,0:T(8,128)(2,1)}, u32[]{:S(2)}) %copy-start.2) | copy-done | bytes 131096
  3.7 0.0 copy-start.3
  3.7 0.9 %copy-done.3 = bf16[256,256]{1,0:T(8,128)(2,1)S(1)} copy-done((bf16[256,256]{1,0:T(8,128)(2,1)S(1)}, bf16[256,256]{1,0:T(8,128)(2,1)}, u32[]{:S(2)}) %copy-start.3) | copy-done | bytes 131096
  4.6 0.0 copy-start.4
  4.6 0.7 copy-done.4
  5.3 61.1 %shard_map.55 = f32[8,2,128]{2,1,0:T(2,128)S(1)} custom-call(f32[16,32768]{1,0:T(8,128)S(1)} %copy-done, bf16[8,256,256]{2,1,0:T(8,128)(2,1)S(1)} %copy-done.1, s32[8]{0:T(128)S(1)} %copy-done.4, bf16[256,256]{1,0:T(8,128)(2,1)S(1)} %copy-done.3, bf16[256,256]{1,0:T(8,128)(2,1)S(1)} %copy-done.2), custom_call_target="tpu_custom_call" | custom-call | tf_op jit(solution)/shard_map/pallas_call | solution.py:413
  66.4 0.6 copy.7
Async XLA Ops:
  0.0 1.6 %copy-start = (f32[16,32768]{1,0:T(8,128)S(1)}, f32[16,32768]{1,0:T(8,128)}, u32[]{:S(2)}) copy-start(f32[16,32768]{1,0:T(8,128)} %x_ref.1) | copy-start | bytes 6291460
  1.6 1.2 %copy-start.1 = (bf16[8,256,256]{2,1,0:T(8,128)(2,1)S(1)}, bf16[8,256,256]{2,1,0:T(8,128)(2,1)}, u32[]{:S(2)}) copy-start(bf16[8,256,256]{2,1,0:T(8,128)(2,1)} %t_ref.1) | copy-start | bytes 3145732
  2.8 0.9 %copy-start.2 = (bf16[256,256]{1,0:T(8,128)(2,1)S(1)}, bf16[256,256]{1,0:T(8,128)(2,1)}, u32[]{:S(2)}) copy-start(bf16[256,256]{1,0:T(8,128)(2,1)} %constant.5.clone.wi_ref) | copy-start | bytes 393220
  3.7 0.9 %copy-start.3 = (bf16[256,256]{1,0:T(8,128)(2,1)S(1)}, bf16[256,256]{1,0:T(8,128)(2,1)}, u32[]{:S(2)}) copy-start(bf16[256,256]{1,0:T(8,128)(2,1)} %constant.4.clone.wf_ref) | copy-start | bytes 393220
  4.6 0.7 copy-start.4

commit v3 on v2

--- a/solution.py
+++ b/solution.py
@@ -54,9 +54,10 @@
 
 
 def kernel(
-    ng, x_ref, t_ref, off_ref, wf_ref, wi_ref, o_ref,
+    ng, x_hbm, t_hbm, off_hbm, tab_hbm, o_ref,
+    x_ref, t_ref, off_ref, tab_ref,
     ys, ws, wz, wv, tsend, trecv, thalo, lhs, band, offv, offs, cb, qb, hs, hr, rs, rr,
-    a_s, a_r, t_s, t_r, f_s, f_r, th_s, th_r, fh_s, fh_r, h_s, h_r, r_s, r_r, loc,
+    a_s, a_r, t_s, t_r, f_s, f_r, th_s, th_r, fh_s, fh_r, h_s, h_r, r_s, r_r, loc, ld,
 ):
     b = lax.axis_index("blk")
     h = lax.axis_index("ch")
@@ -78,6 +79,19 @@
     def far(group):
         return {"blk": GROUP * group + e}
 
+    parts = 4
+    span = x_ref.shape[1] // parts
+
+    def load(i):
+        if i < parts:
+            cols = pl.ds(i * span, span)
+            return pltpu.make_async_copy(x_hbm.at[:, cols], x_ref.at[:, cols], ld.at[i])
+        src, dst = ((off_hbm, off_ref), (t_hbm, t_ref), (tab_hbm, tab_ref))[i - parts]
+        return pltpu.make_async_copy(src, dst, ld.at[i])
+
+    for i in (parts, parts + 1, parts + 2, *range(parts)):
+        load(i).start()
+
     bar = pltpu.get_barrier_semaphore()
 
     def greet_peer(i, carry):
@@ -94,6 +108,8 @@
     r_id = lax.broadcasted_iota(jnp.int32, (256, 256), 0)
     c_id = lax.broadcasted_iota(jnp.int32, (256, 256), 1)
     slot = 128 * ((r_id >> 4) & 1) + 16 * (r_id >> 5) + (r_id & 15)
+    load(parts).wait()
+    load(parts + 1).wait()
     for k in range(TD):
         perm = jnp.where(((slot - c_id - off_ref[k]) & 255) == 0, 1.0, 0.0).astype(BF16)
         placed = jnp.dot(perm, t_ref[k], preferred_element_type=F32).astype(BF16)
@@ -146,7 +162,8 @@
     lax.fori_loop(1, SUBS, start_template, 0)
 
     step = 16
-    wf = wf_ref[...]
+    load(parts + 2).wait()
+    wf = tab_ref[0]
 
     def forward(i, total):
         part = x_ref[:, pl.ds(pl.multiple_of(i * (step * FRAME), FRAME), step * FRAME)]
@@ -156,12 +173,16 @@
         ys[pl.ds(pl.multiple_of(i * (step * CHUNK), 8), step * CHUNK), :] = spec
         return total + jnp.sum((spec * spec).reshape(step, CHUNK, FRAME), axis=0)
 
-    total = lax.fori_loop(0, frames // step, forward, jnp.zeros((CHUNK, FRAME), F32), unroll=8)
+    total = jnp.zeros((CHUNK, FRAME), F32)
+    turns = frames // step // parts
+    for i in range(parts):
+        load(i).wait()
+        total = lax.fori_loop(i * turns, (i + 1) * turns, forward, total, unroll=4)
     mean = total * (1.0 / frames)
     lane = lax.broadcasted_iota(jnp.int32, (CHUNK, FRAME), 1)
     power = jnp.where((lane & 63) == 0, mean, mean + pltpu.roll(mean, 64, 1))
     amp = 1.0 / jnp.sqrt(power + EPS_POWER)
-    wi = wi_ref[...]
+    wi = tab_ref[1]
 
     def sample_copy(t):
         return pltpu.make_async_remote_copy(
@@ -407,15 +428,19 @@
     samples = record.shape[1]
     rows = CHUNK * ng
     buffer = (GROUP + 2) * SLAB
-    wf, wi = transform_tables()
-    vmem = pl.BlockSpec(memory_space=pltpu.VMEM)
+    tables = jnp.asarray(np.stack(transform_tables()))
+    hbm = pl.BlockSpec(memory_space=pl.ANY)
     dma = pltpu.SemaphoreType.DMA
     return pl.pallas_call(
         functools.partial(kernel, ng),
         out_shape=jax.ShapeDtypeStruct((TD, 2, SLAB // 2), F32),
-        in_specs=[vmem, vmem, pl.BlockSpec(memory_space=pltpu.SMEM), vmem, vmem],
-        out_specs=vmem,
+        in_specs=[hbm, hbm, hbm, hbm],
+        out_specs=pl.BlockSpec(memory_space=pltpu.VMEM),
         scratch_shapes=[
+            pltpu.VMEM(record.shape, F32),
+            pltpu.VMEM(templates.shape, BF16),
+            pltpu.SMEM(offsets.shape, jnp.int32),
+            pltpu.VMEM(tables.shape, BF16),
             pltpu.VMEM((samples // FRAME * CHUNK, FRAME), F32),
             pltpu.VMEM((CHUNK, samples), BF16),
             pltpu.VMEM((rows // 32, 32, buffer), BF16),
@@ -435,12 +460,12 @@
             pltpu.VMEM((SUBS, 2, 2, TD, 128), F32),
             dma((ng,)), dma((ng,)), dma((SUBS,)), dma((SUBS,)), dma((GROUP,)), dma((GROUP,)),
             dma((2,)), dma((2,)), dma((2,)), dma((2,)), dma((2,)), dma((2,)), dma((SUBS,)), dma((SUBS,)),
-            dma((1,)),
+            dma((1,)), dma((7,)),
         ],
         compiler_params=pltpu.CompilerParams(
-            collective_id=0, has_side_effects=True, vmem_limit_bytes=48 * 2**20
+            collective_id=0, has_side_effects=True, vmem_limit_bytes=60 * 2**20
         ),
-    )(record, templates, offsets, jnp.asarray(wf), jnp.asarray(wi))
+    )(record, templates, offsets, tables)
 
 
 def solution(mesh):

time: 67.1 us -> 62.9 us (0.937)
  local copies, waits for them, and re-layouts: 5.88 us -> 1.3 us
    unnamed x11 -> x1, local copies, waits for them, and re-layouts: 5.88 us -> 1.3 us
where the time goes in v3:
time: 62.9 us; the launch traced here: 62.8 us
  Pallas kernels  61.5 us (98%)
  local copies, waits for them, and re-layouts  1.3 us (2%)
    pallas_call x1, Pallas kernels, shards(): pl.pallas_call(functools.partial(kernel, ng), out_shape=jax.ShapeDtypeStr...  61.5 us
    unnamed x1, local copies, waits for them, and re-layouts  1.3 us

profile of v3, /device:TPU:1, one launch (start us, length us, event | category | flops | bytes accessed | tf_op | source)
XLA Modules:
  0.0 62.8 jit_solution(5616038857860229232)
XLA Ops:
  0.0 61.5 %shard_map.46 = f32[8,2,128]{2,1,0:T(2,128)} custom-call(f32[16,32768]{1,0:T(8,128)} %x_hbm.1, bf16[8,256,256]{2,1,0:T(8,128)(2,1)} %t_hbm.1, s32[8]{0:T(128)} %off_hbm.1, bf16[2,256,256]{2,1,0:T(8,128)(2,1)} %constant.2.clone.tab_hbm), custom_call_target="tpu_custom_call" | custom-call | tf_op jit(solution)/shard_map/pallas_call | solution.py:434
  61.5 1.3 %copy.6 = f32[8,2,128]{2,1,0:T(2,128)} copy(f32[8,2,128]{2,1,0:T(2,128)} %shard_map.46) | data formatting | bytes 16384

commit v4 on v3

--- a/solution.py
+++ b/solution.py
@@ -33,14 +33,15 @@
     basis = np.where(col <= 64, np.cos(angle), np.sin(angle))
     weight = np.where((col == 0) | (col == 64), 1.0, 2.0) / np.sqrt(FRAME)
 
-    def split(table):
-        high = table.astype(jnp.bfloat16)
-        low = (table - high.astype(np.float64)).astype(jnp.bfloat16)
-        top = np.concatenate([high, low], axis=1)
-        bottom = np.concatenate([high, np.zeros_like(high)], axis=1)
-        return np.concatenate([top, bottom], axis=0)
-
-    return split(basis), split((basis * weight).T)
+    return np.stack([basis, (basis * weight).T]).astype(np.float32)
+
+
+def split_table(table):
+    high = table.astype(BF16)
+    low = (table - high.astype(F32)).astype(BF16)
+    top = jnp.concatenate([high, low], axis=1)
+    bottom = jnp.concatenate([high, jnp.zeros_like(high)], axis=1)
+    return jnp.concatenate([top, bottom], axis=0)
 
 
 def split_rows(value):
@@ -56,7 +57,7 @@
 def kernel(
     ng, x_hbm, t_hbm, off_hbm, tab_hbm, o_ref,
     x_ref, t_ref, off_ref, tab_ref,
-    ys, ws, wz, wv, tsend, trecv, thalo, lhs, band, offv, offs, cb, qb, hs, hr, rs, rr,
+    ys, ws, land, wz, wv, tsend, trecv, thalo, lhs, band, offv, offs, cb, qb, hs, hr, rs, rr,
     a_s, a_r, t_s, t_r, f_s, f_r, th_s, th_r, fh_s, fh_r, h_s, h_r, r_s, r_r, loc, ld,
 ):
     b = lax.axis_index("blk")
@@ -163,7 +164,7 @@
 
     step = 16
     load(parts + 2).wait()
-    wf = tab_ref[0]
+    wf = split_table(tab_ref[0])
 
     def forward(i, total):
         part = x_ref[:, pl.ds(pl.multiple_of(i * (step * FRAME), FRAME), step * FRAME)]
@@ -182,47 +183,50 @@
     lane = lax.broadcasted_iota(jnp.int32, (CHUNK, FRAME), 1)
     power = jnp.where((lane & 63) == 0, mean, mean + pltpu.roll(mean, 64, 1))
     amp = 1.0 / jnp.sqrt(power + EPS_POWER)
-    wi = tab_ref[1]
-
-    def sample_copy(t):
-        return pltpu.make_async_remote_copy(
-            src_ref=ws.at[:, pl.ds(pl.multiple_of(t * wide, FRAME), wide)],
-            dst_ref=wz.at[lax.div(m, 2), pl.ds(half_block(m), CHUNK), pl.ds(SLAB, wide)],
-            send_sem=a_s.at[t], recv_sem=a_r.at[m], device_id=far(t), device_id_type=MESH,
-        )
-
-    def sample_arrival(t):
-        return pltpu.make_async_remote_copy(
-            src_ref=ws.at[:, pl.ds(pl.multiple_of(t * wide, FRAME), wide)],
-            dst_ref=wz.at[lax.div(t, 2), pl.ds(half_block(t), CHUNK), pl.ds(SLAB, wide)],
-            send_sem=a_s.at[t], recv_sem=a_r.at[t], device_id=far(t), device_id_type=MESH,
-        )
-
-    def back(i, carry):
-        pair = lax.rem(lax.div(m, 2) + i, ng // 2)
-        spec = ys[pl.ds(pl.multiple_of(pair * (step * CHUNK), 8), step * CHUNK), :]
-        scaled = (spec.reshape(step, CHUNK, FRAME) * amp[None]).reshape(step * CHUNK, FRAME)
-        both = jnp.dot(split_rows(scaled), wi, preferred_element_type=F32)
-        white = (both[:, :FRAME] + both[:, FRAME:]).astype(BF16)
-        for f in range(step):
-            at = pl.multiple_of((pair * step + f) * FRAME, FRAME)
-            ws[:, pl.ds(at, FRAME)] = white[f * CHUNK : (f + 1) * CHUNK]
-        for q in range(2):
-            t = 2 * pair + q
-
-            @pl.when(t != m)
-            def _():
-                sample_copy(t).start()
-
-        return carry
-
-    lax.fori_loop(0, ng // 2, back, 0, unroll=8)
+    wi = split_table(tab_ref[1])
+
+    def sample_copy(t, wave, source):
+        cols = 2 * SLAB * wave
+        return pltpu.make_async_remote_copy(
+            src_ref=ws.at[:, pl.ds(pl.multiple_of(t * wide + cols, FRAME), 2 * SLAB)],
+            dst_ref=land.at[wave, source],
+            send_sem=a_s.at[wave, t], recv_sem=a_r.at[wave, source], device_id=far(t), device_id_type=MESH,
+        )
+
+    def back(wave):
+        def turn(i, carry):
+            quad = lax.rem(lax.div(m, 4) + i, ng // 4)
+            spec = []
+            for q in range(4):
+                base = (4 * quad + q) * (8 * CHUNK)
+                for first, count in (((0, 2), (6, 2)), ((2, 4),))[wave]:
+                    spec.append(ys[pl.ds(pl.multiple_of(base + first * CHUNK, 8), count * CHUNK), :])
+            spec = jnp.concatenate(spec, axis=0)
+            scaled = (spec.reshape(step, CHUNK, FRAME) * amp[None]).reshape(step * CHUNK, FRAME)
+            both = jnp.dot(split_rows(scaled), wi, preferred_element_type=F32)
+            white = (both[:, :FRAME] + both[:, FRAME:]).astype(BF16)
+            for f in range(step):
+                at = (4 * quad + f // 4) * wide + 2 * SLAB * wave + (f % 4) * FRAME
+                ws[:, pl.ds(pl.multiple_of(at, FRAME), FRAME)] = white[f * CHUNK : (f + 1) * CHUNK]
+            for q in range(4):
+                t = 4 * quad + q
+
+                @pl.when(t != m)
+                def _():
+                    sample_copy(t, wave, m).start()
+
+            return carry
+
+        lax.fori_loop(0, ng // 4, turn, 0, unroll=4)
+        land[wave, m] = ws[
+            :, pl.ds(pl.multiple_of(m * wide + 2 * SLAB * wave, FRAME), 2 * SLAB)
+        ]
+
+    back(0)
 
     wz[:, :, 0:SLAB] = jnp.zeros((rows // 32, 32, SLAB), BF16)
-    wz[:, :, SLAB + wide : 2 * SLAB + wide] = jnp.zeros((rows // 32, 32, SLAB), BF16)
-    wz[lax.div(m, 2), pl.ds(half_block(m), CHUNK), pl.ds(SLAB, wide)] = ws[
-        :, pl.ds(pl.multiple_of(m * wide, FRAME), wide)
-    ]
+    wz[:, :, 5 * SLAB : 6 * SLAB] = jnp.zeros((rows // 32, 32, SLAB), BF16)
+    wv[:, :, 5 * SLAB : 6 * SLAB] = jnp.zeros((rows // 32, 32, SLAB), BF16)
     trecv[d] = tsend[d]
 
     for i in range(1, GROUP):
@@ -254,6 +258,8 @@
         halo(side, "f").start()
         halo(side, "t").start()
 
+    back(1)
+
     w_id = lax.broadcasted_iota(jnp.int32, band.shape, 0)
     l_id = lax.broadcasted_iota(jnp.int32, band.shape, 1)
     gap = w_id - l_id
@@ -295,36 +301,60 @@
     to_scalar.start()
     to_scalar.wait()
 
-    def shift_rows(t):
+    def shift_slabs(t, wave):
         at = pl.ds(half_block(t), CHUNK)
-        block = wz[lax.div(t, 2), at, :]
-        wv[lax.div(t, 2), at, :] = jnp.concatenate([block[:, FOLD:], block[:, :FOLD]], axis=1)
-
-    shift_rows(m)
-
-    def arrive(i, carry):
-        t = lax.rem(m + i, ng)
-        sample_arrival(t).wait()
-        shift_rows(t)
-        return carry
-
-    lax.fori_loop(1, ng, arrive, 0)
-
-    def correlate(shard, k, c0, width):
+        row = lax.div(t, 2)
+
+        block = land[wave, t]
+        new = 1 + 2 * wave
+        wz[row, at, new * SLAB : (new + 2) * SLAB] = block
+        one, two = block[:, :SLAB], block[:, SLAB:]
+
+        def put(i, block, after):
+            wv[row, at, i * SLAB : (i + 1) * SLAB] = jnp.concatenate([block[:, FOLD:], after[:, :FOLD]], axis=1)
+
+        none = jnp.zeros((CHUNK, SLAB), BF16)
+        if wave == 0:
+            put(0, none, one)
+            put(1, one, none)
+            put(2, two, none)
+        else:
+            put(1, wz[row, at, SLAB : 2 * SLAB], one)
+            put(3, one, two)
+            put(4, two, wz[row, at, 2 * SLAB : 3 * SLAB])
+
+    def arrivals(wave):
+        def arrive(i, carry):
+            t = lax.rem(m + i, ng)
+            sample_copy(t, wave, t).wait()
+            shift_slabs(t, wave)
+            return carry
+
+        shift_slabs(m, wave)
+        lax.fori_loop(1, ng, arrive, 0)
+
+    def correlate(shard, k, slabs):
         off = offs[shard, k, 0]
         start = 16 * (off >> 7) + jnp.clip((off & 127) - 16 * d, 0, 16)
         r0 = start >> 5
         r1 = r0 + 1
         r2 = jnp.minimum(r0 + 2, rows // 32 - 1)
-        late = lax.broadcasted_iota(jnp.int32, (32, width), 0) < (start & 31)
-        cols = pl.ds(c0, width)
+        late = lax.broadcasted_iota(jnp.int32, (32, SLAB), 0) < (start & 31)
 
         def window(ref):
-            b0, b1, b2 = ref[r0, :, cols], ref[r1, :, cols], ref[r2, :, cols]
-            return jnp.concatenate([jnp.where(late, b1, b0), jnp.where(late, b2, b1)], axis=0)
+            blocks = []
+            for place in slabs:
+                if place is None:
+                    blocks.append(jnp.zeros((64, SLAB), BF16))
+                    continue
+                cols = pl.ds(place * SLAB, SLAB)
+                b0, b1, b2 = ref[r0, :, cols], ref[r1, :, cols], ref[r2, :, cols]
+                blocks.append(jnp.concatenate([jnp.where(late, b1, b0), jnp.where(late, b2, b1)], axis=0))
+            return jnp.concatenate(blocks, axis=1)
 
         w = window(wz)
         v = window(wv)
+        width = SLAB * len(slabs)
         n = width - 128
         right = jnp.concatenate([w[:, :n], v[:, :n], w[:, 128:], v[:, 128:]], axis=0)
         prod = jnp.dot(lhs[shard * TD + k], right, preferred_element_type=F32)
@@ -345,18 +375,15 @@
         )
         return sums[:TD] + sums[TD : 2 * TD] + sums[2 * TD :]
 
+    arrivals(0)
     for side in range(2):
         shard = (GROUP + 1) * side
-
-        def edge(k, carry):
-            cross, squares = correlate(shard, k, side * wide, 2 * SLAB)
-            cb[shard, k, :, :SLAB] = cross
-            qb[shard, k, :, : 2 * SLAB] = squares
-            return carry
-
-        lax.fori_loop(0, TD, edge, 0, unroll=8)
-        cross = jnp.sum(cb[shard, :, :, :SLAB], axis=1)
-        energy = window_energy(jnp.sum(qb[shard, :, :, : 2 * SLAB], axis=1), 2 * SLAB)
+        for k in range(TD):
+            cross, squares = correlate(shard, k, ((0, 1), (2, None))[side])
+            cb[k, :, :SLAB] = cross
+            qb[k, :, : 2 * SLAB] = squares
+        cross = jnp.sum(cb[:, :, :SLAB], axis=1)
+        energy = window_energy(jnp.sum(qb[:, :, : 2 * SLAB], axis=1), 2 * SLAB)
         if side == 0:
             cross = jnp.where(m == 0, 0.0, cross)
             energy = jnp.where(m == 0, 0.0, energy)
@@ -365,55 +392,53 @@
             hs[side, 1, half] = energy[:, half * 128 : (half + 1) * 128]
         halo(side, "r").start()
 
-    def inner(q, carry):
-        shard = 1 + lax.div(q, TD)
-        k = lax.rem(q, TD)
-        cross, squares = correlate(shard, k, pl.multiple_of((shard - 1) * SLAB, SLAB), 3 * SLAB)
-        cb[shard, k] = cross
-        qb[shard, k] = squares
-        return carry
-
-    lax.fori_loop(0, GROUP * TD, inner, 0, unroll=8)
-
-    def result_copy(sub):
-        return pltpu.make_async_remote_copy(
-            src_ref=rs.at[sub], dst_ref=rr.at[d], send_sem=r_s.at[sub], recv_sem=r_r.at[d],
+    def result_copy(sub, source):
+        return pltpu.make_async_remote_copy(
+            src_ref=rs.at[sub], dst_ref=rr.at[source], send_sem=r_s.at[sub], recv_sem=r_r.at[source],
             device_id=peer(sub), device_id_type=MESH,
         )
 
-    def result_arrival(sub):
-        return pltpu.make_async_remote_copy(
-            src_ref=rs.at[sub], dst_ref=rr.at[sub], send_sem=r_s.at[sub], recv_sem=r_r.at[sub],
-            device_id=peer(sub), device_id_type=MESH,
-        )
-
+    arrivals(1)
     for side in range(2):
         halo(side, "r").wait()
 
-    for own in range(GROUP):
-        cross = jnp.sum(cb[1 + own], axis=1)
-        energy = window_energy(jnp.sum(qb[1 + own], axis=1), 3 * SLAB)
+    def own_shard(own, carry):
+        first = jnp.where(own == 0, 0, jnp.where(own == 1, 1, own + 1))
+        middle = jnp.where(own == 0, 1, jnp.where(own == 3, 2, own + 2))
+        last = jnp.where(own == 0, 3, jnp.where(own == 1, 4, jnp.where(own == 2, 2, 5)))
+        for k in range(TD):
+            cross, squares = correlate(1 + own, k, (first, middle, last))
+            cb[k] = cross
+            qb[k] = squares
+        cross = jnp.sum(cb[...], axis=1)
+        energy = window_energy(jnp.sum(qb[...], axis=1), 3 * SLAB)
         for tile in range(4):
             visit, half = 1 - tile // 2, tile % 2
-            values = [v[:, tile * 128 : (tile + 1) * 128] for v in (cross, energy)]
-            for kind in range(2):
-                value = values[kind]
-                if own == 0 and visit == 1:
-                    value = jnp.where(m == 0, 0.0, value) + hr[1, kind, half]
-                if own == GROUP - 1 and visit == 0:
-                    value = value + hr[0, kind, half]
+            for kind, value in enumerate((cross, energy)):
+                value = value[:, tile * 128 : (tile + 1) * 128]
+                if visit == 1:
+                    value = jnp.where((own == 0) & (m == 0), 0.0, value)
+                    value = value + jnp.where(own == 0, hr[1, kind, half], 0.0)
+                else:
+                    value = value + jnp.where(own == GROUP - 1, hr[0, kind, half], 0.0)
                 rs[2 * own + half, kind, visit] = value
-
-    def start_result(i, carry):
-        result_copy(lax.rem(d + i, SUBS)).start()
-        return carry
+        for half in range(2):
+            sub = 2 * own + half
+
+            @pl.when(sub != d)
+            def _():
+                result_copy(sub, d).start()
+
+        return carry
+
+    lax.fori_loop(0, GROUP, own_shard, 0)
+    rr[d] = rs[d]
 
     def end_result(i, carry):
-        result_arrival(lax.rem(d + i, SUBS)).wait()
-        return carry
-
-    lax.fori_loop(1, SUBS, start_result, 0)
-    rr[d] = rs[d]
+        sub = lax.rem(d + i, SUBS)
+        result_copy(sub, sub).wait()
+        return carry
+
     lax.fori_loop(1, SUBS, end_result, 0)
     summed = rr[0]
     for sub in range(1, SUBS):
@@ -428,7 +453,7 @@
     samples = record.shape[1]
     rows = CHUNK * ng
     buffer = (GROUP + 2) * SLAB
-    tables = jnp.asarray(np.stack(transform_tables()))
+    tables = jnp.asarray(transform_tables())
     hbm = pl.BlockSpec(memory_space=pl.ANY)
     dma = pltpu.SemaphoreType.DMA
     return pl.pallas_call(
@@ -440,9 +465,10 @@
             pltpu.VMEM(record.shape, F32),
             pltpu.VMEM(templates.shape, BF16),
             pltpu.SMEM(offsets.shape, jnp.int32),
-            pltpu.VMEM(tables.shape, BF16),
+            pltpu.VMEM(tables.shape, F32),
             pltpu.VMEM((samples // FRAME * CHUNK, FRAME), F32),
             pltpu.VMEM((CHUNK, samples), BF16),
+            pltpu.VMEM((2, ng, CHUNK, 2 * SLAB), BF16),
             pltpu.VMEM((rows // 32, 32, buffer), BF16),
             pltpu.VMEM((rows // 32, 32, buffer), BF16),
             pltpu.VMEM((SUBS, TD, 32, TLEN), BF16),
@@ -452,13 +478,13 @@
             pltpu.VMEM((3 * SLAB, 2 * SLAB), BF16),
             pltpu.VMEM((GROUP + 2, TD, 128), jnp.int32),
             pltpu.SMEM((GROUP + 2, TD, 128), jnp.int32),
-            pltpu.VMEM((GROUP + 2, TD, 8, 2 * SLAB), F32),
-            pltpu.VMEM((GROUP + 2, TD, 8, 3 * SLAB), F32),
+            pltpu.VMEM((TD, 8, 2 * SLAB), F32),
+            pltpu.VMEM((TD, 8, 3 * SLAB), F32),
             pltpu.VMEM((2, 2, 2, TD, 128), F32),
             pltpu.VMEM((2, 2, 2, TD, 128), F32),
             pltpu.VMEM((SUBS, 2, 2, TD, 128), F32),
             pltpu.VMEM((SUBS, 2, 2, TD, 128), F32),
-            dma((ng,)), dma((ng,)), dma((SUBS,)), dma((SUBS,)), dma((GROUP,)), dma((GROUP,)),
+            dma((2, ng)), dma((2, ng)), dma((SUBS,)), dma((SUBS,)), dma((GROUP,)), dma((GROUP,)),
             dma((2,)), dma((2,)), dma((2,)), dma((2,)), dma((2,)), dma((2,)), dma((SUBS,)), dma((SUBS,)),
             dma((1,)), dma((7,)),
         ],

time: 62.9 us -> 56.1 us (0.89); the launches traced: 62.8 us -> 55.3 us
  Pallas kernels: 61.5 us -> 54 us
    pallas_call x1, Pallas kernels: 61.5 us -> 54 us  [shards(): pl.pallas_call(functools.partial(kernel, ng), out_shape=jax.ShapeDtypeStr...]
where the time goes in v4:
time: 56.1 us; the launch traced here: 55.3 us
  Pallas kernels  54 us (96%)
  local copies, waits for them, and re-layouts  1.3 us (2%)
    pallas_call x1, Pallas kernels, shards(): pl.pallas_call(functools.partial(kernel, ng), out_shape=jax.ShapeDtypeStr...  54 us
    unnamed x1, local copies, waits for them, and re-layouts  1.3 us

profile of v4, /device:TPU:1, one launch (start us, length us, event | category | flops | bytes accessed | tf_op | source)
XLA Modules:
  0.0 55.3 jit_solution(16183772868910992121)
XLA Ops:
  0.0 54.0 %shard_map.46 = f32[8,2,128]{2,1,0:T(2,128)} custom-call(f32[16,32768]{1,0:T(8,128)} %x_hbm.1, bf16[8,256,256]{2,1,0:T(8,128)(2,1)} %t_hbm.1, s32[8]{0:T(128)} %off_hbm.1, f32[2,128,128]{2,1,0:T(8,128)} %constant.2.clone.tab_hbm), custom_call_target="tpu_custom_call" | custom-call | tf_op jit(solution)/shard_map/pallas_call | solution.py:459
  54.0 1.3 %copy.6 = f32[8,2,128]{2,1,0:T(2,128)} copy(f32[8,2,128]{2,1,0:T(2,128)} %shard_map.46) | data formatting | bytes 16384

commit v5 on v4

--- a/solution.py
+++ b/solution.py
@@ -123,8 +123,6 @@
         own_off = jnp.where(row8 == k, off_ref[k], own_off)
     offv[1 + e] = own_off
 
-    pl.semaphore_wait(bar, SUBS - 1 + ng - 1)
-
     def template_copy(i):
         sub = lax.rem(d + i, SUBS)
         return pltpu.make_async_remote_copy(
@@ -153,14 +151,31 @@
             device_id={"blk": GROUP * m + other}, device_id_type=MESH,
         )
 
-    for i in range(1, GROUP):
-        offset_copy(i).start()
-
-    def start_template(i, carry):
-        template_copy(i).start()
-        return carry
-
-    lax.fori_loop(1, SUBS, start_template, 0)
+    def relayed(shard):
+        return (shard == 0) | (shard == GROUP - 1)
+
+    def start_templates(early):
+        @pl.when(relayed(e) == early)
+        def _():
+            def start(i, carry):
+                template_copy(i).start()
+                return carry
+
+            lax.fori_loop(1, SUBS, start, 0)
+
+    def end_templates(early):
+        def end(i, carry):
+            @pl.when(relayed(lax.div(lax.rem(d + i, SUBS), 2)) == early)
+            def _():
+                template_arrival(i).wait_recv()
+
+            @pl.when(relayed(e) == early)
+            def _():
+                template_arrival(i).wait_send()
+
+            return carry
+
+        lax.fori_loop(1, SUBS, end, 0)
 
     step = 16
     load(parts + 2).wait()
@@ -184,6 +199,11 @@
     power = jnp.where((lane & 63) == 0, mean, mean + pltpu.roll(mean, 64, 1))
     amp = 1.0 / jnp.sqrt(power + EPS_POWER)
     wi = split_table(tab_ref[1])
+
+    pl.semaphore_wait(bar, SUBS - 1 + ng - 1)
+    for i in range(1, GROUP):
+        offset_copy(i).start()
+    start_templates(True)
 
     def sample_copy(t, wave, source):
         cols = 2 * SLAB * wave
@@ -232,11 +252,7 @@
     for i in range(1, GROUP):
         offset_arrival(i).wait()
 
-    def end_template(i, carry):
-        template_arrival(i).wait()
-        return carry
-
-    lax.fori_loop(1, SUBS, end_template, 0)
+    end_templates(True)
 
     def halo(side, kind):
         group = up if side == 0 else down
@@ -258,6 +274,7 @@
         halo(side, "f").start()
         halo(side, "t").start()
 
+    start_templates(False)
     back(1)
 
     w_id = lax.broadcasted_iota(jnp.int32, band.shape, 0)
@@ -277,6 +294,8 @@
         spread = jnp.concatenate([both] * 4, axis=0) * keep
         turned = lax.dot_general(pick, spread, (((1,), (1,)), ((), ())), preferred_element_type=F32)
         return turned.astype(BF16)
+
+    end_templates(False)
 
     def prepare(q, carry):
         shard = lax.div(q, TD)

time: 56.1 us -> 52.8 us (0.941); the launches traced: 55.3 us -> 52.6 us
  Pallas kernels: 54 us -> 51.3 us
    pallas_call x1, Pallas kernels: 54 us -> 51.3 us  [shards(): pl.pallas_call(functools.partial(kernel, ng), out_shape=jax.ShapeDtypeStr...]
where the time goes in v5:
time: 52.8 us; the launch traced here: 52.6 us
  Pallas kernels  51.3 us (97%)
  local copies, waits for them, and re-layouts  1.3 us (2%)
    pallas_call x1, Pallas kernels, shards(): pl.pallas_call(functools.partial(kernel, ng), out_shape=jax.ShapeDtypeStr...  51.3 us
    unnamed x1, local copies, waits for them, and re-layouts  1.3 us

profile of v5, /device:TPU:1, one launch (start us, length us, event | category | flops | bytes accessed | tf_op | source)
XLA Modules:
  0.0 52.6 jit_solution(6341169104852312991)
XLA Ops:
  0.0 51.3 %shard_map.46 = f32[8,2,128]{2,1,0:T(2,128)} custom-call(f32[16,32768]{1,0:T(8,128)} %x_hbm.1, bf16[8,256,256]{2,1,0:T(8,128)(2,1)} %t_hbm.1, s32[8]{0:T(128)} %off_hbm.1, f32[2,128,128]{2,1,0:T(8,128)} %constant.2.clone.tab_hbm), custom_call_target="tpu_custom_call" | custom-call | tf_op jit(solution)/shard_map/pallas_call | solution.py:478
  51.3 1.3 %copy.6 = f32[8,2,128]{2,1,0:T(2,128)} copy(f32[8,2,128]{2,1,0:T(2,128)} %shard_map.46) | data formatting | bytes 16384

commit v6 on v5

--- a/solution.py
+++ b/solution.py
@@ -346,11 +346,14 @@
         def arrive(i, carry):
             t = lax.rem(m + i, ng)
             sample_copy(t, wave, t).wait()
+            return carry
+
+        def shift(t, carry):
             shift_slabs(t, wave)
             return carry
 
-        shift_slabs(m, wave)
         lax.fori_loop(1, ng, arrive, 0)
+        lax.fori_loop(0, ng, shift, 0, unroll=8)
 
     def correlate(shard, k, slabs):
         off = offs[shard, k, 0]

time: 52.8 us -> 51.8 us (0.981)
  Pallas kernels: 51.3 us -> 50.3 us
    pallas_call x1, Pallas kernels: 51.3 us -> 50.3 us  [shards(): pl.pallas_call(functools.partial(kernel, ng), out_shape=jax.ShapeDtypeStr...]
where the time goes in v6:
time: 51.8 us; the launch traced here: 51.6 us
  Pallas kernels  50.3 us (97%)
  local copies, waits for them, and re-layouts  1.3 us (3%)
    pallas_call x1, Pallas kernels, shards(): pl.pallas_call(functools.partial(kernel, ng), out_shape=jax.ShapeDtypeStr...  50.3 us
    unnamed x1, local copies, waits for them, and re-layouts  1.3 us

profile of v6, /device:TPU:1, one launch (start us, length us, event | category | flops | bytes accessed | tf_op | source)
XLA Modules:
  0.0 51.6 jit_solution(15826233696462412021)
XLA Ops:
  0.0 50.3 %shard_map.46 = f32[8,2,128]{2,1,0:T(2,128)} custom-call(f32[16,32768]{1,0:T(8,128)} %x_hbm.1, bf16[8,256,256]{2,1,0:T(8,128)(2,1)} %t_hbm.1, s32[8]{0:T(128)} %off_hbm.1, f32[2,128,128]{2,1,0:T(8,128)} %constant.2.clone.tab_hbm), custom_call_target="tpu_custom_call" | custom-call | tf_op jit(solution)/shard_map/pallas_call | solution.py:481
  50.3 1.3 %copy.6 = f32[8,2,128]{2,1,0:T(2,128)} copy(f32[8,2,128]{2,1,0:T(2,128)} %shard_map.46) | data formatting | bytes 16384
